TPU v7x, 128 devices: a whole 4x4x4 slice. The times are simulated.
128 devices in a mesh: grp: 4 (over x_hi, core), blk: 32 (over x_lo, y, z).
Axes of the slice: x: 4 (x_hi: 2, x_lo: 2; x = x_hi * 2 + x_lo), y: 4, z: 4, core: 2. Of those that a mesh axis runs over, the one named last changes fastest.
Arguments:
- queries: bfloat16 [4, 4096, 4096], P('grp', 'blk'), may hold values from -8 to 8
- keys: bfloat16 [4, 4096, 1024], P('grp', 'blk'), may hold values from -6 to 6
- values: bfloat16 [4, 4096, 1024], P('grp', 'blk'), may hold values from -24 to 24
- cache_k: bfloat16 [4, 32, 2, 128, 1024], P('grp', 'blk'), may hold values from -8 to 8
- cache_v: bfloat16 [4, 32, 2, 128, 1024], P('grp', 'blk'), may hold values from -24 to 24
- holder: int32 [32, 4, 1], replicated, may hold values from 0 to 3; in each aligned block of 4 rows (0 to 3, 4 to 7, ..., all dimensions but the last counted through in order) at most 2 rows name the same one
- prefix_len: int32 [4], replicated, may hold values from 1 to 32, 80 in all
Outputs:
- attended: bfloat16 [4, 4096, 4096], P('grp', 'blk')
Inputs may be any that keep to these rules, and one draw needn't show every extreme that they name: Within one column holder[b, :, 0] no index of grp is named more than 2 times, and in some column one is named exactly 2 times. `prefix_len`: some stretch has all 32 blocks.
All inputs are finite; a program needn't handle non-finite values.
Results may differ from a plain program's by a relative error of at most 0.017.
Values may be sent and summed in bfloat16 or wider, within the bound.
A program may use at most 128 MiB of HBM per device.

v0:
```python
import math

import jax
import jax.numpy as jnp
from jax import lax
from jax.sharding import PartitionSpec as P

HEAD_DIM = 128


NEG_FILL = -1e30


def absorb_block(running, queries4, key_part, value_part, visible):
    best_score, weight_sum, weighted = running
    score_scale = queries4.shape[3] ** (-0.5)
    scores = (
        jnp.einsum("tkgd,rkd->tkgr", queries4, key_part, preferred_element_type=jnp.float32)
        * score_scale
    )
    live = visible[:, None, None, :]
    masked = jnp.where(live, scores, NEG_FILL)
    new_best = jnp.maximum(best_score, jnp.max(masked, axis=-1))
    weights = jnp.where(live, jnp.exp(masked - new_best[..., None]), 0.0)
    rescale = jnp.exp(best_score - new_best)
    weight_sum = weight_sum * rescale + jnp.sum(weights, axis=-1)
    weighted = weighted * rescale[..., None] + jnp.einsum(
        "tkgr,rkd->tkgd",
        weights.astype(jnp.bfloat16),
        value_part,
        preferred_element_type=jnp.float32,
    )
    return (new_best, weight_sum, weighted)


def absorb(running, queries4, key_rows, value_rows, visibility):
    key_count = key_rows.shape[0]
    kv_heads = queries4.shape[1]
    head_dim = queries4.shape[3]
    piece_rows = math.gcd(key_count, 512)
    piece_count = key_count // piece_rows
    key_heads = key_rows.reshape(piece_count, piece_rows, kv_heads, head_dim)
    value_heads = value_rows.reshape(piece_count, piece_rows, kv_heads, head_dim)
    offsets = jnp.arange(piece_count, dtype=jnp.int32) * piece_rows

    def step(state_now, element):
        key_part, value_part, offset = element
        key_pos = offset + jnp.arange(piece_rows, dtype=jnp.int32)
        return (absorb_block(state_now, queries4, key_part, value_part, visibility(key_pos)), None)

    running, _ = lax.scan(step, running, (key_heads, value_heads, offsets))
    return running


def local(queries, keys, values, cache_k, cache_v, holder, prefix_len):
    qlocal = queries[0]
    klocal = keys[0]
    vlocal = values[0]
    tok_rows = qlocal.shape[0]
    head_dim = HEAD_DIM
    head_count = qlocal.shape[1] // head_dim
    kv_heads = klocal.shape[1] // head_dim
    group_size = head_count // kv_heads
    groups = lax.axis_size("grp")
    own_block = lax.axis_index("blk")
    own_group = lax.axis_index("grp")
    per_device = holder.shape[1] // groups
    block_rows = cache_k.shape[3]
    column = lax.dynamic_index_in_dim(holder[:, :, 0], own_block, 0, keepdims=False)
    is_held = column == own_group
    slot_ids = jnp.maximum(jnp.cumsum(is_held.astype(jnp.int32)) - 1, 0)
    pool_keys = cache_k[0, 0]
    pool_values = cache_v[0, 0]
    zero_fill = jnp.zeros((), pool_keys.dtype)
    send_keys = jnp.where(is_held[:, None, None], jnp.take(pool_keys, slot_ids, axis=0), zero_fill)
    send_values = jnp.where(
        is_held[:, None, None], jnp.take(pool_values, slot_ids, axis=0), zero_fill
    )
    send_keys = send_keys.reshape(groups, per_device, block_rows, -1)
    send_values = send_values.reshape(groups, per_device, block_rows, -1)
    got_keys, got_values = (
        lax.all_to_all(send_keys, "grp", split_axis=0, concat_axis=0, tiled=True),
        lax.all_to_all(send_values, "grp", split_axis=0, concat_axis=0, tiled=True),
    )
    sources = lax.dynamic_slice_in_dim(column, own_group * per_device, per_device)
    chosen = sources[None, :] == jnp.arange(groups, dtype=jnp.int32)[:, None]
    prefix_keys = jnp.sum(jnp.where(chosen[:, :, None, None], got_keys, zero_fill), axis=0)
    prefix_values = jnp.sum(jnp.where(chosen[:, :, None, None], got_values, zero_fill), axis=0)
    prefix_keys = prefix_keys.reshape(per_device * block_rows, -1)
    prefix_values = prefix_values.reshape(per_device * block_rows, -1)
    key_limit = lax.dynamic_index_in_dim(prefix_len, own_group, 0, keepdims=False) * block_rows
    queries4 = qlocal.reshape(tok_rows, kv_heads, group_size, head_dim)
    query_pos = own_block * tok_rows + jnp.arange(tok_rows, dtype=jnp.int32)

    def prefix_visible(key_pos):
        return jnp.broadcast_to((key_pos < key_limit)[None, :], (tok_rows, key_pos.shape[0]))

    def stretch_visible(key_pos):
        return key_pos[None, :] <= query_pos[:, None]

    start_state = (
        jnp.full((tok_rows, kv_heads, group_size), NEG_FILL, jnp.float32),
        jnp.zeros((tok_rows, kv_heads, group_size), jnp.float32),
        jnp.zeros((tok_rows, kv_heads, group_size, head_dim), jnp.float32),
    )
    pieces = (
        lax.all_gather(prefix_keys, "blk", axis=0, tiled=True),
        lax.all_gather(prefix_values, "blk", axis=0, tiled=True),
    )
    running = absorb(start_state, queries4, pieces[0], pieces[1], prefix_visible)
    pieces = (
        lax.all_gather(klocal, "blk", axis=0, tiled=True),
        lax.all_gather(vlocal, "blk", axis=0, tiled=True),
    )
    best_score, weight_sum, weighted = absorb(
        running, queries4, pieces[0], pieces[1], stretch_visible
    )
    result = (weighted / weight_sum[..., None]).reshape(tok_rows, head_count * head_dim)
    return result.astype(jnp.bfloat16)[None]


def solution(mesh):
    return jax.shard_map(
        local,
        mesh=mesh,
        in_specs=(
            P("grp", "blk", None),
            P("grp", "blk", None),
            P("grp", "blk", None),
            P("grp", "blk", None, None, None),
            P("grp", "blk", None, None, None),
            P(),
            P(),
        ),
        out_specs=P("grp", "blk", None),
        check_vma=False,
    )
```

profile of v0, /device:TPU:0, one launch (start us, length us, event | category | flops | bytes accessed | tf_op | source)
XLA Modules:
  0.0 1039.0 jit_solution(12588101500826201248)
XLA Ops:
  13.6 27.5 %all_to_all.10 = bf16[4,1,128,1024]{3,2,1,0:T(8,128)(2,1)S(1)} all-to-all(bf16[4,1,128,1024]{3,2,1,0:T(8,128)(2,1)S(1)} %get-tuple-element.247), channel_id=1, replica_groups=mesh['grp'=4,'blk'=32] {'grp'}, dimensions={0} | all-to-all | bytes 2097152 | tf_op jit(solution)/shard_map/all_to_all | solution.py:82
  41.2 3.5 all-to-all-start.1
  46.7 24.9 %all-to-all-done.1 = bf16[4,1,128,1024]{3,2,1,0:T(8,128)(2,1)S(1)} async-done(((bf16[4,1,128,1024]{3,2,1,0:T(8,128)(2,1)}), bf16[4,1,128,1024]{3,2,1,0:T(8,128)(2,1)S(1)}, u32[]{:S(2)}, u32[]{:S(2)}) %all-to-all-start.1) | async-done | bytes 1048608 | tf_op jit(solution)/shard_map/all_to_all | solution.py:83
  77.1 110.6 %all-gather.11.cloned.1.call-done = bf16[1,4096,1024]{2,1,0:T(8,128)(2,1)} async-done(((bf16[1,128,1024]{2,1,0:T(8,128)(2,1)}), bf16[1,4096,1024]{2,1,0:T(8,128)(2,1)}) %all-gather.11.cloned.1.call-update) | async-done | bytes 8388624 | tf_op jit(solution)/shard_map/all_gather | solution.py:112
  187.7 8.8 copy.45
  196.5 158.7 %all-gather.13.cloned.1.call-done = bf16[1,4096,1024]{2,1,0:T(8,128)(2,1)} async-done(((bf16[1,128,1024]{2,1,0:T(8,128)(2,1)}), bf16[1,4096,1024]{2,1,0:T(8,128)(2,1)}) %all-gather.13.cloned.1.call-update) | async-done | bytes 8388624 | tf_op jit(solution)/shard_map/all_gather | solution.py:113
  355.2 8.8 copy.46
  364.0 161.1 %all-gather.7.cloned.1.call-done = bf16[4096,1024]{1,0:T(8,128)(2,1)} async-done(((bf16[128,1024]{1,0:T(8,128)(2,1)}), bf16[4096,1024]{1,0:T(8,128)(2,1)}) %all-gather.7.cloned.1.call-update) | async-done | bytes 8388624 | tf_op jit(solution)/shard_map/all_gather | solution.py:107
  525.1 8.8 copy.43
  533.9 161.0 %all-gather.9.cloned.1.call-done = bf16[4096,1024]{1,0:T(8,128)(2,1)} async-done(((bf16[128,1024]{1,0:T(8,128)(2,1)}), bf16[4096,1024]{1,0:T(8,128)(2,1)}) %all-gather.9.cloned.1.call-update) | async-done | bytes 8388624 | tf_op jit(solution)/shard_map/all_gather | solution.py:108
  694.9 8.8 copy.44
  703.6 172.5 %while.31 = (s32[]{:T(128)}, f32[128,8,4]{0,2,1:T(4,128)S(1)}, f32[128,8,4]{0,2,1:T(4,128)S(1)}, f32[128,8,4,128]{0,3,2,1:T(8,128)}, s32[8]{0:T(128)S(1)}, /*ind...) while((s32[]{:T(128)}, f32[128,8,4]{0,2,1:T(4,128)S(1)}, ...), condition=%wide.region_6.8_spmd.clone, body=%wide.region_3.7_spmd.clone.sunk | while | flops 1102599168 | bytes 39061648 | solution.py:51
  706.5 4.6 bitcast_reduce_fusion.2
  711.1 4.6 fusion.54
  717.3 7.4 bitcast_add_fusion.5
  727.6 4.6 bitcast_reduce_fusion.2
  732.2 4.6 fusion.54
  738.3 8.0 bitcast_add_fusion.5
  749.2 4.6 bitcast_reduce_fusion.2
  753.8 4.6 fusion.54
  759.9 8.0 bitcast_add_fusion.5
  770.8 4.6 bitcast_reduce_fusion.2
  775.4 4.6 fusion.54
  781.6 8.0 bitcast_add_fusion.5
  792.5 4.6 bitcast_reduce_fusion.2
  797.1 4.6 fusion.54
  803.2 8.0 bitcast_add_fusion.5
  814.1 4.6 bitcast_reduce_fusion.2
  818.7 4.6 fusion.54
  824.8 8.0 bitcast_add_fusion.5
  835.7 4.6 bitcast_reduce_fusion.2
  840.3 4.6 fusion.54
  846.5 8.0 bitcast_add_fusion.5
  857.4 4.6 bitcast_reduce_fusion.2
  862.0 4.6 fusion.54
  868.1 8.0 bitcast_add_fusion.5
  876.1 153.2 %while.30 = (s32[]{:T(128)}, f32[128,8,4]{0,2,1:T(4,128)S(1)}, f32[128,8,4]{0,2,1:T(4,128)S(1)}, f32[128,8,4,128]{0,3,2,1:T(8,128)}, s32[8]{0:T(128)S(1)}, /*ind...) while((s32[]{:T(128)}, f32[128,8,4]{0,2,1:T(4,128)S(1)}, ...), condition=%wide.region_10.12_spmd.clone, body=%wide.region_7.11_spmd.clone.sunk | while | flops 1102127744 | bytes 72881304 | solution.py:51
  880.6 3.2 copy-done.2
  887.4 7.8 bitcast_add_fusion.4
  899.7 3.2 copy-done.2
  906.6 7.8 bitcast_add_fusion.4
  918.9 3.2 copy-done.2
  925.7 7.8 bitcast_add_fusion.4
  944.9 7.8 bitcast_add_fusion.4
  964.0 7.8 bitcast_add_fusion.4
  983.2 7.8 bitcast_add_fusion.4
  1002.3 7.8 bitcast_add_fusion.4
  1021.5 7.8 bitcast_add_fusion.4
  (191 shorter events, 133.1 us)
Async XLA Ops:
  6.5 2.6 copy-start
  6.5 67.0 %copy-start.3 = (s32[4]{0:T(128)S(1)}, s32[4]{0:T(128)}, u32[]{:S(2)}) copy-start(s32[4]{0:T(128)} %param.19) | copy-start | bytes 52
  6.5 181.1 %all-gather.11.cloned.1.call-start = ((), (), s32[]{:S(2)}) async-start(), calls=%async_computation.4 | async-start | bytes 8650752 | tf_op jit(solution)/shard_map/all_gather | solution.py:112
  7.3 347.9 %all-gather.13.cloned.1.call-start = ((), (), s32[]{:S(2)}) async-start(), calls=%async_computation.5 | async-start | bytes 8650752 | tf_op jit(solution)/shard_map/all_gather | solution.py:113
  41.2 30.4 %all-to-all-start.1 = ((bf16[4,1,128,1024]{3,2,1,0:T(8,128)(2,1)}), bf16[4,1,128,1024]{3,2,1,0:T(8,128)(2,1)S(1)}, u32[]{:S(2)}, u32[]{:S(2)}) async-start(bf16[4,1,128,1024]{3,2,1,0:T(8,128)(2,1)} %get-tuple-element.248), calls=%async_computation.1 | async-start | bytes 2097152 | tf_op jit(solution)/shard_map/all_to_all | solution.py:83
  44.7 480.4 %all-gather.7.cloned.1.call-start = ((), (), s32[]{:S(2)}) async-start(), calls=%async_computation.2 | async-start | bytes 8650752 | tf_op jit(solution)/shard_map/all_gather | solution.py:107
  72.9 621.9 %all-gather.9.cloned.1.call-start = ((), (), s32[]{:S(2)}) async-start(), calls=%async_computation.3 | async-start | bytes 8650752 | tf_op jit(solution)/shard_map/all_gather | solution.py:108
  880.6 3.2 copy-start.2
  899.7 3.2 copy-start.2
  918.9 3.2 copy-start.2
  938.0 3.2 copy-start.2
  957.2 3.2 copy-start.2
  976.3 3.2 copy-start.2
  995.5 3.2 copy-start.2
  1014.6 3.2 copy-start.2
  1029.3 3.2 copy-start.1
Sparse Core Ops, SparseCore 0:
  9.0 178.6 all-gather.10
  189.3 165.8 all-gather.12
  356.8 168.2 all-gather.6
  526.6 168.2 all-gather.8
where the time goes:
time: 1040 us
  waiting for transfers between devices  618 us (59%)
  matrix products  174 us (17%)
  local copies, waits for them, and re-layouts  128 us (12%)
  other arithmetic  73.4 us (7%)
  blocking collectives  27.5 us (3%)
  between operations  13.9 us (1%)
    all_gather x1, waiting for transfers between devices, local(): lax.all_gather(prefix_keys, 'blk', axis=0, tiled=True)  161 us
    all_gather x1, waiting for transfers between devices, local(): lax.all_gather(prefix_values, 'blk', axis=0, tiled=True)  161 us
    all_gather x1, waiting for transfers between devices, local(): lax.all_gather(vlocal, 'blk', axis=0, tiled=True)  159 us
    dot_general x16, matrix products, absorb_block(): jnp.einsum('tkgr,rkd->tkgd', weights.astype(jnp.bfloat16), value_part, pr...  126 us
    all_gather x1, waiting for transfers between devices, local(): lax.all_gather(klocal, 'blk', axis=0, tiled=True)  111 us
    dynamic_slice x48, local copies, waits for them, and re-layouts, absorb(): running, _ = lax.scan(step, running, (key_heads, value_heads, offsets))  59.6 us
    reduce_sum x16, other arithmetic, absorb_block(): weight_sum = weight_sum * rescale + jnp.sum(weights, axis=-1)  54.3 us
    dot_general x16, matrix products, absorb_block(): jnp.einsum('tkgd,rkd->tkgr', queries4, key_part, preferred_element_type=j...  47.9 us
  transfers between devices with their start and end apart: 5, of which 5 were waited for; matrix products, arithmetic and copies ran while one was open for 4% of the time, Pallas kernels for 0%

commit v1 on v0

v1 whole, which is shorter than its diff:
```python
import functools

import jax
import jax.numpy as jnp
from jax import lax
from jax.experimental import pallas as pl
from jax.experimental.pallas import tpu as pltpu
from jax.sharding import PartitionSpec as P

MESH = pl.DeviceIdType.MESH
BF = jnp.bfloat16
F32 = jnp.float32
BIG = 1e30
SCALE = 1.4426950408889634 / (128.0 ** 0.5)


def attend_kernel(
    q_ref, k_ref, v_ref, ck_ref, cv_ref, holder_ref, plen_ref, o_ref,
    kv, q_in, q_hi, q_lo, acc, top, s0, s1, ob,
    skv, sib_out, sib_in, cand, pc, pens,
    s_sib, r_sib, s_st, r_st, s_q, r_q, s_p, r_p, s_z, r_z, s_f, r_f, s_o, r_o,
):
    g = lax.axis_index("grp")
    b = lax.axis_index("blk")
    xh, core = g // 2, g % 2
    h, z = b // 4, b % 4

    def plane(d):
        return (g, ((h + d) % 8) * 4 + z)

    def across(d):
        return ((1 - xh) * 2 + core, ((h + d) % 8) * 4 + z)

    sibling = (xh * 2 + 1 - core, b)
    z_up = (g, h * 4 + (z + 1) % 4)
    z_down = (g, h * 4 + (z + 3) % 4)

    barrier = pltpu.get_barrier_semaphore()
    peers = [plane(d) for d in range(1, 8)] + [across(d) for d in range(8)] + [sibling, z_up, z_down]
    for peer in peers:
        pl.semaphore_signal(barrier, inc=1, device_id=peer, device_id_type=MESH)

    def remote(src, dst, send, recv, peer):
        return pltpu.make_async_remote_copy(
            src_ref=src, dst_ref=dst, send_sem=send, recv_sem=recv, device_id=peer, device_id_type=MESH
        )

    def held(c):
        own = holder_ref[b, c]
        slot = jnp.int32(0)
        for c2 in range(4):
            slot = slot + jnp.where((c2 < c) & (holder_ref[b, c2] == own), 1, 0)
        return own, jnp.minimum(slot, 1)

    for e in range(2):
        _, slot = held(2 * e + 1 - core)
        sib_out[e, 0] = ck_ref[slot]
        sib_out[e, 1] = cv_ref[slot]
    for p in range(8):
        lanes = slice(p * 128, (p + 1) * 128)
        skv[p, 0] = k_ref[:, lanes]
        skv[p, 1] = v_ref[:, lanes].T
    plen = plen_ref[g]
    for c in range(4, 8):
        for n in range(8):
            u, k = n // 4, n % 4
            if c == 4:
                block = 4 * n + z
            elif c == 7:
                block = 4 * n + (z + 2) % 4
            else:
                block = 4 * (4 * (c - 5) + k) + (z + (3 if u == 0 else 1)) % 4
            pens[c, n] = jnp.where(block < plen, 0.0, BIG)
    for c in range(4):
        for n in range(8):
            pens[c, n] = 0.0
    top[...] = jnp.full(top.shape, -BIG, F32)
    acc[...] = jnp.zeros(acc.shape, F32)

    pl.semaphore_wait(barrier, len(peers))

    sib_copy = remote(sib_out, sib_in, s_sib.at[0], r_sib.at[0], sibling)
    sib_copy.start()
    st_copies, q_copies, p_copies = [], [], []
    for d in range(1, 8):
        to = (h + d) % 8
        copy = remote(skv.at[to], kv.at[h // 2, h % 2, 0], s_st.at[d], r_st.at[d], plane(d))
        copy.start()
        st_copies.append(copy)
    for d in range(1, 8):
        to = (h + d) % 8
        lanes = pl.ds(pl.multiple_of(to * 512, 512), 512)
        copy = remote(q_ref.at[:, lanes], q_in.at[h], s_q.at[d], r_q.at[d], plane(d))
        copy.start()
        q_copies.append(copy)
    kv[h // 2, h % 2, 0] = skv[h]
    q_in[h] = q_ref[:, pl.ds(pl.multiple_of(h * 512, 512), 512)]

    sib_copy.wait_recv()
    for e in range(2):
        own, slot = held(2 * e + core)
        from_sibling = own == xh * 2 + 1 - core
        for p in range(8):
            lanes = slice(p * 128, (p + 1) * 128)
            cand[e, p, 0] = jnp.where(from_sibling, sib_in[e, 0, :, lanes], ck_ref[slot, :, lanes])
            cand[e, p, 1] = jnp.where(from_sibling, sib_in[e, 1, :, lanes], cv_ref[slot, :, lanes])
    for d in range(8):
        to = (h + d) % 8
        copy = remote(cand.at[1 - xh, to], pc.at[xh, h], s_p.at[8 + d], r_p.at[8 + d], across(d))
        copy.start()
        p_copies.append(copy)
        if d:
            copy = remote(cand.at[xh, to], pc.at[xh, h], s_p.at[d], r_p.at[d], plane(d))
            copy.start()
            p_copies.append(copy)
    pc[xh, h] = cand[xh, h]

    for copy in st_copies:
        copy.wait_recv()

    def stretch_up(j):
        return remote(kv.at[j, :, 0], kv.at[j, :, 1], s_z.at[j, 0], r_z.at[j, 0], z_up)

    def stretch_down(j):
        return remote(kv.at[j, :, 0], kv.at[j, :, 3], s_z.at[j, 1], r_z.at[j, 1], z_down)

    def stretch_on_up(j):
        return remote(kv.at[j, :, 1, 0], kv.at[j, :, 2, 0], s_f.at[j, 0], r_f.at[j, 0], z_up)

    def stretch_on_down(j):
        return remote(kv.at[j, :, 3, 1], kv.at[j, :, 2, 1], s_f.at[j, 1], r_f.at[j, 1], z_down)

    def prefix_up(u):
        return remote(kv.at[4, u], kv.at[5 + u, 0], s_z.at[4 + u, 0], r_z.at[4 + u, 0], z_up)

    def prefix_down(u):
        return remote(kv.at[4, u], kv.at[5 + u, 1], s_z.at[4 + u, 1], r_z.at[4 + u, 1], z_down)

    def prefix_on_up(u):
        return remote(kv.at[5 + u, 0, :, 0], kv.at[7, u, :, 0], s_f.at[4 + u, 0], r_f.at[4 + u, 0], z_up)

    def prefix_on_down(u):
        return remote(kv.at[5 + u, 1, :, 1], kv.at[7, u, :, 1], s_f.at[4 + u, 1], r_f.at[4 + u, 1], z_down)

    for j in range(4):
        stretch_up(j).start()
        stretch_down(j).start()

    def forward_stretch(j):
        stretch_up(j).wait_recv()
        stretch_on_up(j).start()
        stretch_down(j).wait_recv()
        stretch_on_down(j).start()

    forward_stretch(0)

    def prepare(i, _):
        for m in range(4):
            x = q_in[i, :, m * 128 : (m + 1) * 128].astype(F32) * SCALE
            hi = x.astype(BF)
            rows = slice(m * 128, (m + 1) * 128)
            q_hi[i, rows] = hi
            q_lo[i, rows] = (x - hi.astype(F32)).astype(BF)
        return 0

    for copy in q_copies:
        copy.wait_recv()
    lax.fori_loop(0, 8, prepare, 0)

    def scores(c, i):
        keys = kv[c, :, :, 0].reshape(1024, 128)
        queries = jnp.concatenate([q_hi[i], q_lo[i]], axis=1)
        keys = jnp.concatenate([keys, keys], axis=1)
        return lax.dot_general(keys, queries, (((1,), (1,)), ((), ())), preferred_element_type=F32)

    def soften(s_ref, c, i, blocks, pen, corner=None):
        parts = []
        best = top[i]
        for n in range(blocks):
            part = s_ref[n * 128 : (n + 1) * 128, :]
            if n == corner:
                key_at = lax.broadcasted_iota(jnp.int32, (128, 512), 0)
                query_at = lax.broadcasted_iota(jnp.int32, (128, 512), 1) % 128
                part = jnp.where(key_at <= query_at, part, -BIG)
            parts.append(part)
            high = jnp.max(part, axis=0, keepdims=True)
            if pen[n] is not None:
                high = high - pen[n]
            best = jnp.maximum(best, high)
        fade = jnp.exp2(top[i] - best)
        top[i] = best
        weights = []
        for n in range(blocks):
            base = best if pen[n] is None else best + pen[n]
            weights.append(jnp.exp2(parts[n] - base).astype(BF))
        weights = jnp.concatenate(weights, axis=0)
        values_t = jnp.concatenate([kv[c, n // 4, n % 4, 1] for n in range(blocks)], axis=1)
        values_t = jnp.concatenate([values_t, jnp.ones((16, blocks * 128), BF)], axis=0)
        acc[i] = acc[i] * fade + jnp.dot(values_t, weights, preferred_element_type=F32)

    def pair(c, t, c_next, t_next):
        pen = [pens[c, n] for n in range(8)]
        s1[...] = scores(c, 2 * t + 1)
        soften(s0, c, 2 * t, 8, pen)
        s0[...] = scores(c_next, 2 * t_next)
        soften(s1, c, 2 * t + 1, 8, pen)

    later = [jnp.where(r <= z, 0.0, BIG) for r in range(4)]

    def diagonal(t):
        s1[...] = scores(t, 2 * t + 1)
        soften(s0, t, 2 * t, 4, [None] + later[1:], corner=0)
        soften(s1, t, 2 * t + 1, 8, [None] * 5 + later[1:], corner=4)

    def stretch_run(t, _):
        @pl.when(t < 3)
        def _():
            forward_stretch(t + 1)

        stretch_on_up(t).wait_recv()
        stretch_on_down(t).wait_recv()
        s0[...] = scores(0, 2 * t)

        def inner(j, _):
            pair(j, t, j + 1, t)
            return 0

        lax.fori_loop(0, t, inner, 0)
        diagonal(t)
        return 0

    lax.fori_loop(0, 4, stretch_run, 0)

    for copy in p_copies:
        copy.wait_recv()

    def pick(n, _):
        side = holder_ref[4 * n + z, g] // 2
        kv[4, n // 4, n % 4, 0] = pc[side, n, 0]
        kv[4, n // 4, n % 4, 1] = pc[side, n, 1].T
        return 0

    lax.fori_loop(0, 8, pick, 0)
    for u in range(2):
        prefix_up(u).start()
        prefix_down(u).start()

    def forward_prefix(u):
        prefix_up(u).wait_recv()
        prefix_on_up(u).start()
        prefix_down(u).wait_recv()
        prefix_on_down(u).start()

    def chunk_run(c, _):
        @pl.when(c == 5)
        def _():
            forward_prefix(0)

        s0[...] = scores(c, 0)

        def inner(t, _):
            pair(c, t, c, (t + 1) % 4)
            return 0

        lax.fori_loop(0, 4, inner, 0)
        return 0

    lax.fori_loop(4, 6, chunk_run, 0)
    forward_prefix(1)
    for u in range(2):
        prefix_on_up(u).wait_recv()
        prefix_on_down(u).wait_recv()

    mine = pl.ds(pl.multiple_of(h * 512, 512), 512)

    def out_copy(i):
        return remote(ob.at[i], o_ref.at[:, mine], s_o.at[i], r_o.at[h], (g, i * 4 + z))

    def own_copy(i):
        return pltpu.make_async_copy(ob.at[i], o_ref.at[:, mine], s_o.at[i])

    def finish(i):
        total = acc[i]
        out = total[0:128] / total[128:129]
        for m in range(4):
            lanes = slice(m * 128, (m + 1) * 128)
            ob[i, :, lanes] = out[:, lanes].T.astype(BF)

        @pl.when(i != h)
        def _():
            out_copy(i).start()

        @pl.when(i == h)
        def _():
            own_copy(i).start()

    def last_run(t, _):
        s0[...] = scores(6, 2 * t)

        def inner(c, _):
            pair(c, t, 7, t)
            return 0

        lax.fori_loop(6, 8, inner, 0)
        finish(2 * t)
        finish(2 * t + 1)
        return 0

    lax.fori_loop(0, 4, last_run, 0)

    sib_copy.wait_send()
    for copy in st_copies + q_copies + p_copies:
        copy.wait_send()
    for j in range(4):
        for copy in (stretch_up(j), stretch_down(j), stretch_on_up(j), stretch_on_down(j)):
            copy.wait_send()
    for u in range(2):
        for copy in (prefix_up(u), prefix_down(u), prefix_on_up(u), prefix_on_down(u)):
            copy.wait_send()

    def settle(i, _):
        @pl.when(i != h)
        def _():
            out_copy(i).wait_send()
            lanes = pl.ds(pl.multiple_of(i * 512, 512), 512)
            remote(ob.at[i], o_ref.at[:, lanes], s_o.at[i], r_o.at[i], (g, i * 4 + z)).wait_recv()

        @pl.when(i == h)
        def _():
            own_copy(i).wait()

        return 0

    lax.fori_loop(0, 8, settle, 0)


def local(queries, keys, values, cache_k, cache_v, holder, prefix_len):
    vmem = pl.BlockSpec(memory_space=pltpu.VMEM)
    smem = pl.BlockSpec(memory_space=pltpu.SMEM)
    dma = pltpu.SemaphoreType.DMA
    out = pl.pallas_call(
        attend_kernel,
        out_shape=jax.ShapeDtypeStruct((128, 4096), BF),
        in_specs=[vmem, vmem, vmem, vmem, vmem, smem, smem],
        out_specs=pl.BlockSpec(memory_space=pl.ANY),
        scratch_shapes=[
            pltpu.VMEM((8, 2, 4, 2, 128, 128), BF),
            pltpu.VMEM((8, 128, 512), BF),
            pltpu.VMEM((8, 512, 128), BF),
            pltpu.VMEM((8, 512, 128), BF),
            pltpu.VMEM((8, 144, 512), F32),
            pltpu.VMEM((8, 1, 512), F32),
            pltpu.VMEM((1024, 512), F32),
            pltpu.VMEM((1024, 512), F32),
            pltpu.VMEM((8, 128, 512), BF),
            pltpu.VMEM((8, 2, 128, 128), BF),
            pltpu.VMEM((2, 2, 128, 1024), BF),
            pltpu.VMEM((2, 2, 128, 1024), BF),
            pltpu.VMEM((2, 8, 2, 128, 128), BF),
            pltpu.VMEM((2, 8, 2, 128, 128), BF),
            pltpu.SMEM((8, 8), F32),
            dma((1,)), dma((1,)),
            dma((8,)), dma((8,)),
            dma((8,)), dma((8,)),
            dma((16,)), dma((16,)),
            dma((6, 2)), dma((6, 2)),
            dma((6, 2)), dma((6, 2)),
            dma((8,)), dma((8,)),
        ],
        compiler_params=pltpu.CompilerParams(
            collective_id=0, has_side_effects=True, vmem_limit_bytes=56 * 2**20
        ),
        cost_estimate=pl.CostEstimate(flops=14 * 10**9, bytes_accessed=4 * 2**20, transcendentals=27 * 10**6),
        name="attend",
    )(
        queries[0], keys[0], values[0], cache_k[0, 0], cache_v[0, 0], holder[:, :, 0], prefix_len,
    )
    return out[None]


def solution(mesh):
    return jax.shard_map(
        local,
        mesh=mesh,
        in_specs=(
            P("grp", "blk", None),
            P("grp", "blk", None),
            P("grp", "blk", None),
            P("grp", "blk", None, None, None),
            P("grp", "blk", None, None, None),
            P(),
            P(),
        ),
        out_specs=P("grp", "blk", None),
        check_vma=False,
    )
```

time: 1040 us -> 99.3 us (0.10)
  waiting for transfers between devices: 618 us -> 0 us
  matrix products: 174 us -> 0 us
  local copies, waits for them, and re-layouts: 128 us -> 3.66 us
  Pallas kernels: 0 us -> 94.7 us
  other arithmetic: 73.4 us -> 0 us
  blocking collectives: 27.5 us -> 0 us
  between operations: 13.9 us -> 0.01 us
    all_gather x4 -> x0, waiting for transfers between devices: 591 us -> none  [the longest x1 161 us: local(): lax.all_gather(prefix_keys, 'blk', axis=0, tiled=True)]
    dot_general x32 -> x0, matrix products: 174 us -> none  [the longest x16 126 us: absorb_block(): jnp.einsum('tkgr,rkd->tkgd', weights.astype(jnp.bfloat16), value_part, pr...]
    pallas_call x0 -> x1, Pallas kernels: none -> 94.7 us  [local(): pl.pallas_call(attend_kernel, out_shape=jax.ShapeDtypeStruct((128, 4096),...]
    dynamic_slice x50 -> x0, local copies, waits for them, and re-layouts: 61.5 us -> none  [the longest x48 59.6 us: absorb(): running, _ = lax.scan(step, running, (key_heads, value_heads, offsets))]
    reduce_sum x17 -> x0, other arithmetic: 55.6 us -> none  [the longest x16 54.3 us: absorb_block(): weight_sum = weight_sum * rescale + jnp.sum(weights, axis=-1)]
    unnamed x12 -> x3, local copies, waits for them, and re-layouts: 37.4 us -> 2.97 us
    all_to_all x1 -> x0, blocking collectives: 27.5 us -> none  [local(): lax.all_to_all(send_keys, 'grp', split_axis=0, concat_axis=0, tiled=True)]
    while x32 -> x0, local copies, waits for them, and re-layouts: 25.7 us -> none
  transfers between devices with their start and end apart: 5 -> 0, of which waited for: 5 -> 0; matrix products, arithmetic and copies ran while one was open for 4% -> 0% of each run, Pallas kernels for 0% -> 0%
where the time goes in v1:
time: 99.3 us; the launch traced here: 98.4 us
  Pallas kernels  94.7 us (95%)
  local copies, waits for them, and re-layouts  3.66 us (4%)
    pallas_call x1, Pallas kernels, local(): pl.pallas_call(attend_kernel, out_shape=jax.ShapeDtypeStruct((128, 4096),...  94.7 us
    unnamed x3, local copies, waits for them, and re-layouts  2.97 us

profile of v1, /device:TPU:0, one launch (start us, length us, event | category | flops | bytes accessed | tf_op | source)
XLA Modules:
  0.0 98.4 jit_solution(12725075707667942879)
XLA Ops:
  0.0 0.0 copy-start
  0.0 0.7 copy-done
  0.7 0.7 copy.8.holder_ref
  1.4 94.7 %attend.1 = bf16[128,4096]{1,0:T(8,128)(2,1)} custom-call(bf16[128,4096]{1,0:T(8,128)(2,1)} %bitcast.9, bf16[128,1024]{1,0:T(8,128)(2,1)} %bitcast.12, bf16[128,1024]{1,0:T(8,128)(2,1)} %bitcast.13, bf16[2,128,1024]{2,1,0:T(8,128)(2,1)} %bitcast.10, bf16[2,128,1024]{2,1,0:T(8,128)(2,1)} %bitcast.11, s32[32,4]{1,0:T(8,128)} %copy.8.holder_ref, s32[4]{0:T(128)} %plen_ref.1), custom_call_target="tpu_custom_call" | custom-call | flops 14000000000 | bytes 4194304 | tf_op jit(solution)/shard_map/attend/pallas_call | solution.py:341
  96.1 2.3 %copy.10 = bf16[1,128,4096]{2,1,0:T(8,128)(2,1)} copy(bf16[1,128,4096]{2,1,0:T(8,128)(2,1)} %bitcast.7) | data formatting | bytes 2097152
Async XLA Ops:
  0.0 0.7 copy-start

commit v2 on v1

--- a/solution.py
+++ b/solution.py
@@ -12,12 +12,13 @@
 F32 = jnp.float32
 BIG = 1e30
 SCALE = 1.4426950408889634 / (128.0 ** 0.5)
+ORDER = (4, 1, 3, 5, 7, 6, 2)
 
 
 def attend_kernel(
     q_ref, k_ref, v_ref, ck_ref, cv_ref, holder_ref, plen_ref, o_ref,
-    kv, q_in, q_hi, q_lo, acc, top, s0, s1, ob,
-    skv, sib_out, sib_in, cand, pc, pens,
+    kv, q_in, acc, top, s0, s1, ob,
+    skv, sib_out, sib_in, cand, pc_k, pc_v, pens,
     s_sib, r_sib, s_st, r_st, s_q, r_q, s_p, r_p, s_z, r_z, s_f, r_f, s_o, r_o,
 ):
     g = lax.axis_index("grp")
@@ -25,11 +26,14 @@
     xh, core = g // 2, g % 2
     h, z = b // 4, b % 4
 
+    def turned(d):
+        return ((h // 4 + d // 4) % 2) * 4 + (h % 4 + d % 4) % 4
+
     def plane(d):
-        return (g, ((h + d) % 8) * 4 + z)
+        return (g, turned(d) * 4 + z)
 
     def across(d):
-        return ((1 - xh) * 2 + core, ((h + d) % 8) * 4 + z)
+        return ((1 - xh) * 2 + core, turned(d) * 4 + z)
 
     sibling = (xh * 2 + 1 - core, b)
     z_up = (g, h * 4 + (z + 1) % 4)
@@ -63,13 +67,7 @@
     plen = plen_ref[g]
     for c in range(4, 8):
         for n in range(8):
-            u, k = n // 4, n % 4
-            if c == 4:
-                block = 4 * n + z
-            elif c == 7:
-                block = 4 * n + (z + 2) % 4
-            else:
-                block = 4 * (4 * (c - 5) + k) + (z + (3 if u == 0 else 1)) % 4
+            block = 4 * n + (z + (0, 3, 1, 2)[c - 4]) % 4
             pens[c, n] = jnp.where(block < plen, 0.0, BIG)
     for c in range(4):
         for n in range(8):
@@ -81,14 +79,14 @@
 
     sib_copy = remote(sib_out, sib_in, s_sib.at[0], r_sib.at[0], sibling)
     sib_copy.start()
-    st_copies, q_copies, p_copies = [], [], []
-    for d in range(1, 8):
-        to = (h + d) % 8
+    st_copies, q_copies, p_copies = [], [], ([], [])
+    for d in ORDER:
+        to = turned(d)
         copy = remote(skv.at[to], kv.at[h // 2, h % 2, 0], s_st.at[d], r_st.at[d], plane(d))
         copy.start()
         st_copies.append(copy)
-    for d in range(1, 8):
-        to = (h + d) % 8
+    for d in ORDER:
+        to = turned(d)
         lanes = pl.ds(pl.multiple_of(to * 512, 512), 512)
         copy = remote(q_ref.at[:, lanes], q_in.at[h], s_q.at[d], r_q.at[d], plane(d))
         copy.start()
@@ -97,23 +95,23 @@
     q_in[h] = q_ref[:, pl.ds(pl.multiple_of(h * 512, 512), 512)]
 
     sib_copy.wait_recv()
-    for e in range(2):
-        own, slot = held(2 * e + core)
-        from_sibling = own == xh * 2 + 1 - core
-        for p in range(8):
-            lanes = slice(p * 128, (p + 1) * 128)
-            cand[e, p, 0] = jnp.where(from_sibling, sib_in[e, 0, :, lanes], ck_ref[slot, :, lanes])
-            cand[e, p, 1] = jnp.where(from_sibling, sib_in[e, 1, :, lanes], cv_ref[slot, :, lanes])
-    for d in range(8):
-        to = (h + d) % 8
-        copy = remote(cand.at[1 - xh, to], pc.at[xh, h], s_p.at[8 + d], r_p.at[8 + d], across(d))
-        copy.start()
-        p_copies.append(copy)
-        if d:
-            copy = remote(cand.at[xh, to], pc.at[xh, h], s_p.at[d], r_p.at[d], plane(d))
+    for n, cache in ((0, ck_ref), (1, cv_ref)):
+        for e in range(2):
+            own, slot = held(2 * e + core)
+            from_sibling = own == xh * 2 + 1 - core
+            for p in range(8):
+                lanes = slice(p * 128, (p + 1) * 128)
+                cand[n, e, p] = jnp.where(from_sibling, sib_in[e, n, :, lanes], cache[slot, :, lanes])
+        for d in (0,) + ORDER:
+            to = turned(d)
+            copy = remote(cand.at[n, 1 - xh, to], (pc_k, pc_v)[n].at[xh, h], s_p.at[n, 8 + d], r_p.at[n, 8 + d], across(d))
             copy.start()
-            p_copies.append(copy)
-    pc[xh, h] = cand[xh, h]
+            p_copies[n].append(copy)
+            if d:
+                copy = remote(cand.at[n, xh, to], (pc_k, pc_v)[n].at[xh, h], s_p.at[n, d], r_p.at[n, d], plane(d))
+                copy.start()
+                p_copies[n].append(copy)
+        (pc_k, pc_v)[n][xh, h] = cand[n, xh, h]
 
     for copy in st_copies:
         copy.wait_recv()
@@ -130,19 +128,19 @@
     def stretch_on_down(j):
         return remote(kv.at[j, :, 3, 1], kv.at[j, :, 2, 1], s_f.at[j, 1], r_f.at[j, 1], z_down)
 
-    def prefix_up(u):
-        return remote(kv.at[4, u], kv.at[5 + u, 0], s_z.at[4 + u, 0], r_z.at[4 + u, 0], z_up)
-
-    def prefix_down(u):
-        return remote(kv.at[4, u], kv.at[5 + u, 1], s_z.at[4 + u, 1], r_z.at[4 + u, 1], z_down)
-
-    def prefix_on_up(u):
-        return remote(kv.at[5 + u, 0, :, 0], kv.at[7, u, :, 0], s_f.at[4 + u, 0], r_f.at[4 + u, 0], z_up)
-
-    def prefix_on_down(u):
-        return remote(kv.at[5 + u, 1, :, 1], kv.at[7, u, :, 1], s_f.at[4 + u, 1], r_f.at[4 + u, 1], z_down)
-
-    for j in range(4):
+    def prefix_up(n):
+        return remote(kv.at[4, :, :, n], kv.at[5, :, :, n], s_z.at[4 + n, 0], r_z.at[4 + n, 0], z_up)
+
+    def prefix_down(n):
+        return remote(kv.at[4, :, :, n], kv.at[6, :, :, n], s_z.at[4 + n, 1], r_z.at[4 + n, 1], z_down)
+
+    def prefix_on_up():
+        return remote(kv.at[5, :, :, 0], kv.at[7, :, :, 0], s_f.at[4, 0], r_f.at[4, 0], z_up)
+
+    def prefix_on_down():
+        return remote(kv.at[6, :, :, 1], kv.at[7, :, :, 1], s_f.at[4, 1], r_f.at[4, 1], z_down)
+
+    def send_stretch(j):
         stretch_up(j).start()
         stretch_down(j).start()
 
@@ -152,25 +150,29 @@
         stretch_down(j).wait_recv()
         stretch_on_down(j).start()
 
-    forward_stretch(0)
-
-    def prepare(i, _):
-        for m in range(4):
-            x = q_in[i, :, m * 128 : (m + 1) * 128].astype(F32) * SCALE
-            hi = x.astype(BF)
-            rows = slice(m * 128, (m + 1) * 128)
-            q_hi[i, rows] = hi
-            q_lo[i, rows] = (x - hi.astype(F32)).astype(BF)
-        return 0
+    def pick(n):
+        for copy in p_copies[n]:
+            copy.wait_recv()
+        for i in range(8):
+            side = holder_ref[4 * i + z, g] // 2
+            part = (pc_k, pc_v)[n][side, i]
+            kv[4, i // 4, i % 4, n] = part.T if n else part
+        prefix_up(n).start()
+        prefix_down(n).start()
+
+    send_stretch(0)
+    send_stretch(1)
+    for j in range(3):
+        forward_stretch(j)
+        if j < 2:
+            send_stretch(j + 2)
 
     for copy in q_copies:
         copy.wait_recv()
-    lax.fori_loop(0, 8, prepare, 0)
 
     def scores(c, i):
         keys = kv[c, :, :, 0].reshape(1024, 128)
-        queries = jnp.concatenate([q_hi[i], q_lo[i]], axis=1)
-        keys = jnp.concatenate([keys, keys], axis=1)
+        queries = jnp.concatenate([q_in[i, :, m * 128 : (m + 1) * 128] for m in range(4)], axis=0)
         return lax.dot_general(keys, queries, (((1,), (1,)), ((), ())), preferred_element_type=F32)
 
     def soften(s_ref, c, i, blocks, pen, corner=None):
@@ -187,12 +189,12 @@
             if pen[n] is not None:
                 high = high - pen[n]
             best = jnp.maximum(best, high)
-        fade = jnp.exp2(top[i] - best)
+        fade = jnp.exp2((top[i] - best) * SCALE)
         top[i] = best
         weights = []
         for n in range(blocks):
             base = best if pen[n] is None else best + pen[n]
-            weights.append(jnp.exp2(parts[n] - base).astype(BF))
+            weights.append(jnp.exp2((parts[n] - base) * SCALE).astype(BF))
         weights = jnp.concatenate(weights, axis=0)
         values_t = jnp.concatenate([kv[c, n // 4, n % 4, 1] for n in range(blocks)], axis=1)
         values_t = jnp.concatenate([values_t, jnp.ones((16, blocks * 128), BF)], axis=0)
@@ -213,15 +215,23 @@
         soften(s1, t, 2 * t + 1, 8, [None] * 5 + later[1:], corner=4)
 
     def stretch_run(t, _):
-        @pl.when(t < 3)
-        def _():
-            forward_stretch(t + 1)
-
         stretch_on_up(t).wait_recv()
         stretch_on_down(t).wait_recv()
         s0[...] = scores(0, 2 * t)
 
+        @pl.when(t == 1)
+        def _():
+            forward_stretch(3)
+
         def inner(j, _):
+            @pl.when((t == 2) & (j == 1))
+            def _():
+                pick(0)
+
+            @pl.when((t == 3) & (j == 2))
+            def _():
+                pick(1)
+
             pair(j, t, j + 1, t)
             return 0
 
@@ -231,30 +241,16 @@
 
     lax.fori_loop(0, 4, stretch_run, 0)
 
-    for copy in p_copies:
-        copy.wait_recv()
-
-    def pick(n, _):
-        side = holder_ref[4 * n + z, g] // 2
-        kv[4, n // 4, n % 4, 0] = pc[side, n, 0]
-        kv[4, n // 4, n % 4, 1] = pc[side, n, 1].T
-        return 0
-
-    lax.fori_loop(0, 8, pick, 0)
-    for u in range(2):
-        prefix_up(u).start()
-        prefix_down(u).start()
-
-    def forward_prefix(u):
-        prefix_up(u).wait_recv()
-        prefix_on_up(u).start()
-        prefix_down(u).wait_recv()
-        prefix_on_down(u).start()
+    prefix_up(0).wait_recv()
+    prefix_on_up().start()
+    prefix_down(0).wait_recv()
 
     def chunk_run(c, _):
         @pl.when(c == 5)
         def _():
-            forward_prefix(0)
+            prefix_down(1).wait_recv()
+            prefix_on_down().start()
+            prefix_up(1).wait_recv()
 
         s0[...] = scores(c, 0)
 
@@ -266,10 +262,8 @@
         return 0
 
     lax.fori_loop(4, 6, chunk_run, 0)
-    forward_prefix(1)
-    for u in range(2):
-        prefix_on_up(u).wait_recv()
-        prefix_on_down(u).wait_recv()
+    prefix_on_up().wait_recv()
+    prefix_on_down().wait_recv()
 
     mine = pl.ds(pl.multiple_of(h * 512, 512), 512)
 
@@ -294,7 +288,8 @@
         def _():
             own_copy(i).start()
 
-    def last_run(t, _):
+    def last_run(n, _):
+        t = (h // 2 + 1 + n) % 4
         s0[...] = scores(6, 2 * t)
 
         def inner(c, _):
@@ -309,14 +304,13 @@
     lax.fori_loop(0, 4, last_run, 0)
 
     sib_copy.wait_send()
-    for copy in st_copies + q_copies + p_copies:
+    for copy in st_copies + q_copies + p_copies[0] + p_copies[1]:
         copy.wait_send()
     for j in range(4):
         for copy in (stretch_up(j), stretch_down(j), stretch_on_up(j), stretch_on_down(j)):
             copy.wait_send()
-    for u in range(2):
-        for copy in (prefix_up(u), prefix_down(u), prefix_on_up(u), prefix_on_down(u)):
-            copy.wait_send()
+    for copy in (prefix_up(0), prefix_down(0), prefix_up(1), prefix_down(1), prefix_on_up(), prefix_on_down()):
+        copy.wait_send()
 
     def settle(i, _):
         @pl.when(i != h)
@@ -346,8 +340,6 @@
         scratch_shapes=[
             pltpu.VMEM((8, 2, 4, 2, 128, 128), BF),
             pltpu.VMEM((8, 128, 512), BF),
-            pltpu.VMEM((8, 512, 128), BF),
-            pltpu.VMEM((8, 512, 128), BF),
             pltpu.VMEM((8, 144, 512), F32),
             pltpu.VMEM((8, 1, 512), F32),
             pltpu.VMEM((1024, 512), F32),
@@ -356,13 +348,14 @@
             pltpu.VMEM((8, 2, 128, 128), BF),
             pltpu.VMEM((2, 2, 128, 1024), BF),
             pltpu.VMEM((2, 2, 128, 1024), BF),
-            pltpu.VMEM((2, 8, 2, 128, 128), BF),
-            pltpu.VMEM((2, 8, 2, 128, 128), BF),
+            pltpu.VMEM((2, 2, 8, 128, 128), BF),
+            pltpu.VMEM((2, 8, 128, 128), BF),
+            pltpu.VMEM((2, 8, 128, 128), BF),
             pltpu.SMEM((8, 8), F32),
             dma((1,)), dma((1,)),
             dma((8,)), dma((8,)),
             dma((8,)), dma((8,)),
-            dma((16,)), dma((16,)),
+            dma((2, 16)), dma((2, 16)),
             dma((6, 2)), dma((6, 2)),
             dma((6, 2)), dma((6, 2)),
             dma((8,)), dma((8,)),

time: 99.3 us -> 82 us (0.83)
  Pallas kernels: 94.7 us -> 78.2 us
    pallas_call x1, Pallas kernels: 94.7 us -> 78.2 us  [local(): pl.pallas_call(attend_kernel, out_shape=jax.ShapeDtypeStruct((128, 4096),...]
where the time goes in v2:
time: 82 us; the launch traced here: 81.8 us
  Pallas kernels  78.2 us (95%)
  local copies, waits for them, and re-layouts  3.66 us (4%)
    pallas_call x1, Pallas kernels, local(): pl.pallas_call(attend_kernel, out_shape=jax.ShapeDtypeStruct((128, 4096),...  78.2 us
    unnamed x3, local copies, waits for them, and re-layouts  2.97 us

profile of v2, /device:TPU:0, one launch (start us, length us, event | category | flops | bytes accessed | tf_op | source)
XLA Modules:
  0.0 81.8 jit_solution(14503366401983437829)
XLA Ops:
  0.0 0.0 copy-start
  0.0 0.7 copy-done
  0.7 0.7 copy.8.holder_ref
  1.4 78.2 %attend.1 = bf16[128,4096]{1,0:T(8,128)(2,1)} custom-call(bf16[128,4096]{1,0:T(8,128)(2,1)} %bitcast.9, bf16[128,1024]{1,0:T(8,128)(2,1)} %bitcast.12, bf16[128,1024]{1,0:T(8,128)(2,1)} %bitcast.13, bf16[2,128,1024]{2,1,0:T(8,128)(2,1)} %bitcast.10, bf16[2,128,1024]{2,1,0:T(8,128)(2,1)} %bitcast.11, s32[32,4]{1,0:T(8,128)} %copy.8.holder_ref, s32[4]{0:T(128)} %plen_ref.1), custom_call_target="tpu_custom_call" | custom-call | flops 14000000000 | bytes 4194304 | tf_op jit(solution)/shard_map/attend/pallas_call | solution.py:335
  79.6 2.3 %copy.10 = bf16[1,128,4096]{2,1,0:T(8,128)(2,1)} copy(bf16[1,128,4096]{2,1,0:T(8,128)(2,1)} %bitcast.7) | data formatting | bytes 2097152
Async XLA Ops:
  0.0 0.7 copy-start

commit v3 on v2

--- a/solution.py
+++ b/solution.py
@@ -13,13 +13,14 @@
 BIG = 1e30
 SCALE = 1.4426950408889634 / (128.0 ** 0.5)
 ORDER = (4, 1, 3, 5, 7, 6, 2)
+LAST = (6, 2, 5, 7, 1, 3, 4, 0)
 
 
 def attend_kernel(
     q_ref, k_ref, v_ref, ck_ref, cv_ref, holder_ref, plen_ref, o_ref,
     kv, q_in, acc, top, s0, s1, ob,
-    skv, sib_out, sib_in, cand, pc_k, pc_v, pens,
-    s_sib, r_sib, s_st, r_st, s_q, r_q, s_p, r_p, s_z, r_z, s_f, r_f, s_o, r_o,
+    skv, sib_out, sib_in, cand, pc_k, pc_v, k_in, v_in, ck_in, cv_in, pens,
+    s_in, s_sib, r_sib, s_st, r_st, s_q, r_q, s_p, r_p, s_z, r_z, s_f, r_f, s_zp, r_zp, s_fp, r_fp, s_o, r_o,
 ):
     g = lax.axis_index("grp")
     b = lax.axis_index("blk")
@@ -50,35 +51,31 @@
         )
 
     def held(c):
-        own = holder_ref[b, c]
+        own = holder_ref[c, b]
         slot = jnp.int32(0)
         for c2 in range(4):
-            slot = slot + jnp.where((c2 < c) & (holder_ref[b, c2] == own), 1, 0)
+            slot = slot + jnp.where((c2 < c) & (holder_ref[c2, b] == own), 1, 0)
         return own, jnp.minimum(slot, 1)
 
-    for e in range(2):
-        _, slot = held(2 * e + 1 - core)
-        sib_out[e, 0] = ck_ref[slot]
-        sib_out[e, 1] = cv_ref[slot]
+    fetches = [
+        pltpu.make_async_copy(src, dst, s_in.at[n])
+        for n, (src, dst) in enumerate(((k_ref, k_in), (v_ref, v_in), (ck_ref, ck_in), (cv_ref, cv_in)))
+    ]
+    for fetch in fetches:
+        fetch.start()
+    own_queries = pltpu.make_async_copy(
+        q_ref.at[:, pl.ds(pl.multiple_of(h * 512, 512), 512)], q_in.at[h], s_in.at[4]
+    )
+    own_queries.start()
+    fetches[0].wait()
+    fetches[1].wait()
     for p in range(8):
         lanes = slice(p * 128, (p + 1) * 128)
-        skv[p, 0] = k_ref[:, lanes]
-        skv[p, 1] = v_ref[:, lanes].T
-    plen = plen_ref[g]
-    for c in range(4, 8):
-        for n in range(8):
-            block = 4 * n + (z + (0, 3, 1, 2)[c - 4]) % 4
-            pens[c, n] = jnp.where(block < plen, 0.0, BIG)
-    for c in range(4):
-        for n in range(8):
-            pens[c, n] = 0.0
-    top[...] = jnp.full(top.shape, -BIG, F32)
-    acc[...] = jnp.zeros(acc.shape, F32)
+        skv[p, 0] = k_in[:, lanes]
+        skv[p, 1] = v_in[:, lanes].T
 
     pl.semaphore_wait(barrier, len(peers))
 
-    sib_copy = remote(sib_out, sib_in, s_sib.at[0], r_sib.at[0], sibling)
-    sib_copy.start()
     st_copies, q_copies, p_copies = [], [], ([], [])
     for d in ORDER:
         to = turned(d)
@@ -91,11 +88,32 @@
         copy = remote(q_ref.at[:, lanes], q_in.at[h], s_q.at[d], r_q.at[d], plane(d))
         copy.start()
         q_copies.append(copy)
+
+    fetches[2].wait()
+    fetches[3].wait()
+    for e in range(2):
+        _, slot = held(2 * e + 1 - core)
+        sib_out[e, 0] = ck_in[slot]
+        sib_out[e, 1] = cv_in[slot]
+    sib_copy = remote(sib_out, sib_in, s_sib.at[0], r_sib.at[0], sibling)
+    sib_copy.start()
     kv[h // 2, h % 2, 0] = skv[h]
-    q_in[h] = q_ref[:, pl.ds(pl.multiple_of(h * 512, 512), 512)]
+    plen = plen_ref[g]
+    for c in range(4, 8):
+        for n in range(8):
+            if c in (4, 7):
+                block = 4 * n + (z + 2 * (c // 7)) % 4
+            else:
+                block = 4 * (4 * (c - 5) + n % 4) + (z + 3 - 2 * (n // 4)) % 4
+            pens[c, n] = jnp.where(block < plen, 0.0, BIG)
+    for c in range(4):
+        for n in range(8):
+            pens[c, n] = 0.0
+    top[...] = jnp.full(top.shape, -BIG, F32)
+    acc[...] = jnp.zeros(acc.shape, F32)
 
     sib_copy.wait_recv()
-    for n, cache in ((0, ck_ref), (1, cv_ref)):
+    for n, cache in ((0, ck_in), (1, cv_in)):
         for e in range(2):
             own, slot = held(2 * e + core)
             from_sibling = own == xh * 2 + 1 - core
@@ -128,17 +146,22 @@
     def stretch_on_down(j):
         return remote(kv.at[j, :, 3, 1], kv.at[j, :, 2, 1], s_f.at[j, 1], r_f.at[j, 1], z_down)
 
-    def prefix_up(n):
-        return remote(kv.at[4, :, :, n], kv.at[5, :, :, n], s_z.at[4 + n, 0], r_z.at[4 + n, 0], z_up)
-
-    def prefix_down(n):
-        return remote(kv.at[4, :, :, n], kv.at[6, :, :, n], s_z.at[4 + n, 1], r_z.at[4 + n, 1], z_down)
-
-    def prefix_on_up():
-        return remote(kv.at[5, :, :, 0], kv.at[7, :, :, 0], s_f.at[4, 0], r_f.at[4, 0], z_up)
-
-    def prefix_on_down():
-        return remote(kv.at[6, :, :, 1], kv.at[7, :, :, 1], s_f.at[4, 1], r_f.at[4, 1], z_down)
+    def prefix_up(n, u):
+        return remote(kv.at[4, u, :, n], kv.at[5 + u, 0, :, n], s_zp.at[n, u, 0], r_zp.at[n, u, 0], z_up)
+
+    def prefix_down(n, u):
+        return remote(kv.at[4, u, :, n], kv.at[5 + u, 1, :, n], s_zp.at[n, u, 1], r_zp.at[n, u, 1], z_down)
+
+    def prefix_on(n, u):
+        return remote(kv.at[5 + u, n, :, n], kv.at[7, u, :, n], s_fp.at[n, u], r_fp.at[n, u], (z_up, z_down)[n])
+
+    def forward_prefix(n, u):
+        prefix_up(n, u).wait_recv()
+        if n == 0:
+            prefix_on(n, u).start()
+        prefix_down(n, u).wait_recv()
+        if n == 1:
+            prefix_on(n, u).start()
 
     def send_stretch(j):
         stretch_up(j).start()
@@ -154,11 +177,12 @@
         for copy in p_copies[n]:
             copy.wait_recv()
         for i in range(8):
-            side = holder_ref[4 * i + z, g] // 2
+            side = holder_ref[g, 4 * i + z] // 2
             part = (pc_k, pc_v)[n][side, i]
             kv[4, i // 4, i % 4, n] = part.T if n else part
-        prefix_up(n).start()
-        prefix_down(n).start()
+        for u in range(2):
+            prefix_up(n, u).start()
+            prefix_down(n, u).start()
 
     send_stretch(0)
     send_stretch(1)
@@ -169,6 +193,7 @@
 
     for copy in q_copies:
         copy.wait_recv()
+    own_queries.wait()
 
     def scores(c, i):
         keys = kv[c, :, :, 0].reshape(1024, 128)
@@ -200,70 +225,90 @@
         values_t = jnp.concatenate([values_t, jnp.ones((16, blocks * 128), BF)], axis=0)
         acc[i] = acc[i] * fade + jnp.dot(values_t, weights, preferred_element_type=F32)
 
-    def pair(c, t, c_next, t_next):
+    def pair(c, a, b, c_next, a_next):
         pen = [pens[c, n] for n in range(8)]
-        s1[...] = scores(c, 2 * t + 1)
-        soften(s0, c, 2 * t, 8, pen)
-        s0[...] = scores(c_next, 2 * t_next)
-        soften(s1, c, 2 * t + 1, 8, pen)
+        s1[...] = scores(c, b)
+        soften(s0, c, a, 8, pen)
+        s0[...] = scores(c_next, a_next)
+        soften(s1, c, b, 8, pen)
 
     later = [jnp.where(r <= z, 0.0, BIG) for r in range(4)]
 
     def diagonal(t):
         s1[...] = scores(t, 2 * t + 1)
         soften(s0, t, 2 * t, 4, [None] + later[1:], corner=0)
+        s0[...] = scores(jnp.where(t == 3, 4, t), (2 * t + 2) % 8)
         soften(s1, t, 2 * t + 1, 8, [None] * 5 + later[1:], corner=4)
 
-    def stretch_run(t, _):
-        stretch_on_up(t).wait_recv()
-        stretch_on_down(t).wait_recv()
-        s0[...] = scores(0, 2 * t)
-
-        @pl.when(t == 1)
-        def _():
-            forward_stretch(3)
-
-        def inner(j, _):
-            @pl.when((t == 2) & (j == 1))
+    def gathered(j):
+        stretch_on_up(j).wait_recv()
+        stretch_on_down(j).wait_recv()
+
+    def stretch_run(j, _):
+        @pl.when(j == 3)
+        def _():
+            pick(1)
+
+        diagonal(j)
+
+        def inner(t, _):
+            @pl.when((j == 0) & (t == 2))
+            def _():
+                forward_stretch(3)
+
+            @pl.when((j == 1) & (t == 2))
             def _():
                 pick(0)
 
-            @pl.when((t == 3) & (j == 2))
+            @pl.when(t == 3)
             def _():
-                pick(1)
-
-            pair(j, t, j + 1, t)
+                gathered(j + 1)
+
+            last = t == 3
+            j_next = jnp.where(last, j + 1, j)
+            pair(j, 2 * t, 2 * t + 1, j_next, jnp.where(last, 2 * j + 2, 2 * t + 2))
             return 0
 
-        lax.fori_loop(0, t, inner, 0)
-        diagonal(t)
+        lax.fori_loop(j + 1, 4, inner, 0)
         return 0
 
+    gathered(0)
+    s0[...] = scores(0, 0)
     lax.fori_loop(0, 4, stretch_run, 0)
 
-    prefix_up(0).wait_recv()
-    prefix_on_up().start()
-    prefix_down(0).wait_recv()
+    def last_tile(n):
+        step = jnp.int32(LAST[7])
+        for m in range(7):
+            step = jnp.where(n % 8 == m, LAST[m], step)
+        return turned(step)
 
     def chunk_run(c, _):
         @pl.when(c == 5)
         def _():
-            prefix_down(1).wait_recv()
-            prefix_on_down().start()
-            prefix_up(1).wait_recv()
-
-        s0[...] = scores(c, 0)
+            forward_prefix(1, 0)
 
         def inner(t, _):
-            pair(c, t, c, (t + 1) % 4)
+            @pl.when((c == 4) & (t == 2))
+            def _():
+                forward_prefix(0, 0)
+                forward_prefix(0, 1)
+
+            @pl.when((c == 5) & (t == 3))
+            def _():
+                forward_prefix(1, 1)
+
+            last = t == 3
+            a_next = jnp.where(last & (c == 5), last_tile(0), (2 * t + 2) % 8)
+            pair(c, 2 * t, 2 * t + 1, jnp.where(last, c + 1, c), a_next)
             return 0
 
         lax.fori_loop(0, 4, inner, 0)
         return 0
 
     lax.fori_loop(4, 6, chunk_run, 0)
-    prefix_on_up().wait_recv()
-    prefix_on_down().wait_recv()
+    for n in range(2):
+        for u in range(2):
+            prefix_on(n, u).wait_recv()
 
     mine = pl.ds(pl.multiple_of(h * 512, 512), 512)
 
@@ -289,19 +334,16 @@
             own_copy(i).start()
 
     def last_run(n, _):
-        t = (h // 2 + 1 + n) % 4
-        s0[...] = scores(6, 2 * t)
-
-        def inner(c, _):
-            pair(c, t, 7, t)
-            return 0
-
-        lax.fori_loop(6, 8, inner, 0)
-        finish(2 * t)
-        finish(2 * t + 1)
+        i = last_tile(n)
+        pen = [[pens[c, m] for m in range(8)] for c in (6, 7)]
+        s1[...] = scores(7, i)
+        soften(s0, 6, i, 8, pen[0])
+        s0[...] = scores(6, last_tile(n + 1))
+        soften(s1, 7, i, 8, pen[1])
+        finish(i)
         return 0
 
-    lax.fori_loop(0, 4, last_run, 0)
+    lax.fori_loop(0, 8, last_run, 0)
 
     sib_copy.wait_send()
     for copy in st_copies + q_copies + p_copies[0] + p_copies[1]:
@@ -309,8 +351,10 @@
     for j in range(4):
         for copy in (stretch_up(j), stretch_down(j), stretch_on_up(j), stretch_on_down(j)):
             copy.wait_send()
-    for copy in (prefix_up(0), prefix_down(0), prefix_up(1), prefix_down(1), prefix_on_up(), prefix_on_down()):
-        copy.wait_send()
+    for n in range(2):
+        for u in range(2):
+            for copy in (prefix_up(n, u), prefix_down(n, u), prefix_on(n, u)):
+                copy.wait_send()
 
     def settle(i, _):
         @pl.when(i != h)
@@ -329,14 +373,14 @@
 
 
 def local(queries, keys, values, cache_k, cache_v, holder, prefix_len):
-    vmem = pl.BlockSpec(memory_space=pltpu.VMEM)
+    hbm = pl.BlockSpec(memory_space=pl.ANY)
     smem = pl.BlockSpec(memory_space=pltpu.SMEM)
     dma = pltpu.SemaphoreType.DMA
     out = pl.pallas_call(
         attend_kernel,
         out_shape=jax.ShapeDtypeStruct((128, 4096), BF),
-        in_specs=[vmem, vmem, vmem, vmem, vmem, smem, smem],
-        out_specs=pl.BlockSpec(memory_space=pl.ANY),
+        in_specs=[hbm] * 5 + [smem, smem],
+        out_specs=hbm,
         scratch_shapes=[
             pltpu.VMEM((8, 2, 4, 2, 128, 128), BF),
             pltpu.VMEM((8, 128, 512), BF),
@@ -351,13 +395,20 @@
             pltpu.VMEM((2, 2, 8, 128, 128), BF),
             pltpu.VMEM((2, 8, 128, 128), BF),
             pltpu.VMEM((2, 8, 128, 128), BF),
+            pltpu.VMEM((128, 1024), BF),
+            pltpu.VMEM((128, 1024), BF),
+            pltpu.VMEM((2, 128, 1024), BF),
+            pltpu.VMEM((2, 128, 1024), BF),
             pltpu.SMEM((8, 8), F32),
+            dma((5,)),
             dma((1,)), dma((1,)),
             dma((8,)), dma((8,)),
             dma((8,)), dma((8,)),
             dma((2, 16)), dma((2, 16)),
-            dma((6, 2)), dma((6, 2)),
-            dma((6, 2)), dma((6, 2)),
+            dma((4, 2)), dma((4, 2)),
+            dma((4, 2)), dma((4, 2)),
+            dma((2, 2, 2)), dma((2, 2, 2)),
+            dma((2, 2)), dma((2, 2)),
             dma((8,)), dma((8,)),
         ],
         compiler_params=pltpu.CompilerParams(
@@ -366,7 +417,7 @@
         cost_estimate=pl.CostEstimate(flops=14 * 10**9, bytes_accessed=4 * 2**20, transcendentals=27 * 10**6),
         name="attend",
     )(
-        queries[0], keys[0], values[0], cache_k[0, 0], cache_v[0, 0], holder[:, :, 0], prefix_len,
+        queries[0], keys[0], values[0], cache_k[0, 0], cache_v[0, 0], holder[:, :, 0].T, prefix_len,
     )
     return out[None]
 

time: 82 us -> 75.7 us (0.923)
  Pallas kernels: 78.2 us -> 72.7 us
  local copies, waits for them, and re-layouts: 3.66 us -> 2.29 us
    pallas_call x1, Pallas kernels: 78.2 us -> 72.7 us  [local(): pl.pallas_call(attend_kernel, out_shape=jax.ShapeDtypeStruct((128, 4096),...]
    unnamed x3 -> x1, local copies, waits for them, and re-layouts: 2.97 us -> 2.29 us
where the time goes in v3:
time: 75.7 us; the launch traced here: 75 us
  Pallas kernels  72.7 us (96%)
  local copies, waits for them, and re-layouts  2.29 us (3%)
    pallas_call x1, Pallas kernels, local(): pl.pallas_call(attend_kernel, out_shape=jax.ShapeDtypeStruct((128, 4096),...  72.7 us
    unnamed x1, local copies, waits for them, and re-layouts  2.29 us

profile of v3, /device:TPU:0, one launch (start us, length us, event | category | flops | bytes accessed | tf_op | source)
XLA Modules:
  0.0 75.0 jit_solution(6015517054582173883)
XLA Ops:
  0.0 72.7 %attend.1 = bf16[128,4096]{1,0:T(8,128)(2,1)} custom-call(bf16[128,4096]{1,0:T(8,128)(2,1)} %bitcast.10, bf16[128,1024]{1,0:T(8,128)(2,1)} %bitcast.13, bf16[128,1024]{1,0:T(8,128)(2,1)} %bitcast.14, bf16[2,128,1024]{2,1,0:T(8,128)(2,1)} %bitcast.11, bf16[2,128,1024]{2,1,0:T(8,128)(2,1)} %bitcast.12, s32[4,32]{1,0:T(4,128)} %bitcast.15, s32[4]{0:T(128)} %plen_ref.1), custom_call_target="tpu_custom_call" | custom-call | flops 14000000000 | bytes 4194304 | tf_op jit(solution)/shard_map/attend/pallas_call | solution.py:379
  72.7 2.3 %copy.9 = bf16[1,128,4096]{2,1,0:T(8,128)(2,1)} copy(bf16[1,128,4096]{2,1,0:T(8,128)(2,1)} %bitcast.9) | data formatting | bytes 2097152

commit v4 on v3

--- a/solution.py
+++ b/solution.py
@@ -112,14 +112,14 @@
     top[...] = jnp.full(top.shape, -BIG, F32)
     acc[...] = jnp.zeros(acc.shape, F32)
 
-    sib_copy.wait_recv()
-    for n, cache in ((0, ck_in), (1, cv_in)):
+    def send_prefix(n, cache):
         for e in range(2):
             own, slot = held(2 * e + core)
             from_sibling = own == xh * 2 + 1 - core
             for p in range(8):
                 lanes = slice(p * 128, (p + 1) * 128)
-                cand[n, e, p] = jnp.where(from_sibling, sib_in[e, n, :, lanes], cache[slot, :, lanes])
+                part = jnp.where(from_sibling, sib_in[e, n, :, lanes], cache[slot, :, lanes])
+                cand[n, e, p] = part.T if n else part
         for d in (0,) + ORDER:
             to = turned(d)
             copy = remote(cand.at[n, 1 - xh, to], (pc_k, pc_v)[n].at[xh, h], s_p.at[n, 8 + d], r_p.at[n, 8 + d], across(d))
@@ -131,9 +131,6 @@
                 p_copies[n].append(copy)
         (pc_k, pc_v)[n][xh, h] = cand[n, xh, h]
 
-    for copy in st_copies:
-        copy.wait_recv()
-
     def stretch_up(j):
         return remote(kv.at[j, :, 0], kv.at[j, :, 1], s_z.at[j, 0], r_z.at[j, 0], z_up)
 
@@ -153,15 +150,13 @@
         return remote(kv.at[4, u, :, n], kv.at[5 + u, 1, :, n], s_zp.at[n, u, 1], r_zp.at[n, u, 1], z_down)
 
     def prefix_on(n, u):
-        return remote(kv.at[5 + u, n, :, n], kv.at[7, u, :, n], s_fp.at[n, u], r_fp.at[n, u], (z_up, z_down)[n])
+        return remote(kv.at[5 + u, u, :, n], kv.at[7, u, :, n], s_fp.at[n, u], r_fp.at[n, u], (z_up, z_down)[u])
 
     def forward_prefix(n, u):
-        prefix_up(n, u).wait_recv()
-        if n == 0:
-            prefix_on(n, u).start()
-        prefix_down(n, u).wait_recv()
-        if n == 1:
-            prefix_on(n, u).start()
+        here, other = (prefix_up, prefix_down) if u == 0 else (prefix_down, prefix_up)
+        here(n, u).wait_recv()
+        prefix_on(n, u).start()
+        other(n, u).wait_recv()
 
     def send_stretch(j):
         stretch_up(j).start()
@@ -178,14 +173,18 @@
             copy.wait_recv()
         for i in range(8):
             side = holder_ref[g, 4 * i + z] // 2
-            part = (pc_k, pc_v)[n][side, i]
-            kv[4, i // 4, i % 4, n] = part.T if n else part
+            kv[4, i // 4, i % 4, n] = (pc_k, pc_v)[n][side, i]
         for u in range(2):
             prefix_up(n, u).start()
             prefix_down(n, u).start()
 
+    sib_copy.wait_recv()
+    send_prefix(0, ck_in)
+    for copy in st_copies:
+        copy.wait_recv()
     send_stretch(0)
     send_stretch(1)
+    send_prefix(1, cv_in)
     for j in range(3):
         forward_stretch(j)
         if j < 2:
@@ -256,7 +255,7 @@
             def _():
                 forward_stretch(3)
 
-            @pl.when((j == 1) & (t == 2))
+            @pl.when((j == 0) & (t == 3))
             def _():
                 pick(0)
 
@@ -378,9 +377,9 @@
     dma = pltpu.SemaphoreType.DMA
     out = pl.pallas_call(
         attend_kernel,
-        out_shape=jax.ShapeDtypeStruct((128, 4096), BF),
+        out_shape=pltpu.VMEM((128, 4096), BF),
         in_specs=[hbm] * 5 + [smem, smem],
-        out_specs=hbm,
+        out_specs=pl.BlockSpec(memory_space=pltpu.VMEM),
         scratch_shapes=[
             pltpu.VMEM((8, 2, 4, 2, 128, 128), BF),
             pltpu.VMEM((8, 128, 512), BF),

time: 75.7 us -> 73.1 us (0.966)
  local copies, waits for them, and re-layouts: 2.29 us -> 0.97 us
    unnamed x1, local copies, waits for them, and re-layouts: 2.29 us -> 0.97 us
where the time goes in v4:
time: 73.1 us; the launch traced here: 73 us
  Pallas kernels  72 us (98%)
  local copies, waits for them, and re-layouts  0.97 us (1%)
    pallas_call x1, Pallas kernels, local(): pl.pallas_call(attend_kernel, out_shape=pltpu.VMEM((128, 4096), BF), in_s...  72 us

profile of v4, /device:TPU:0, one launch (start us, length us, event | category | flops | bytes accessed | tf_op | source)
XLA Modules:
  0.0 73.0 jit_solution(4450707953519866332)
XLA Ops:
  0.0 72.0 %attend.1 = bf16[128,4096]{1,0:T(8,128)(2,1)S(1)} custom-call(bf16[128,4096]{1,0:T(8,128)(2,1)} %bitcast.10, bf16[128,1024]{1,0:T(8,128)(2,1)} %bitcast.13, bf16[128,1024]{1,0:T(8,128)(2,1)} %bitcast.14, bf16[2,128,1024]{2,1,0:T(8,128)(2,1)} %bitcast.11, bf16[2,128,1024]{2,1,0:T(8,128)(2,1)} %bitcast.12, s32[4,32]{1,0:T(4,128)} %bitcast.15, s32[4]{0:T(128)} %plen_ref.1), custom_call_target="tpu_custom_call" | custom-call | flops 14000000000 | bytes 4194304 | tf_op jit(solution)/shard_map/attend/pallas_call | solution.py:378
  72.0 1.0 %copy.9 = bf16[1,128,4096]{2,1,0:T(8,128)(2,1)} copy(bf16[1,128,4096]{2,1,0:T(8,128)(2,1)S(1)} %bitcast.9) | data formatting | bytes 2097152

commit v5 on v4

--- a/solution.py
+++ b/solution.py
@@ -13,7 +13,7 @@
 BIG = 1e30
 SCALE = 1.4426950408889634 / (128.0 ** 0.5)
 ORDER = (4, 1, 3, 5, 7, 6, 2)
-LAST = (6, 2, 5, 7, 1, 3, 4, 0)
+LAST = (6, 2, 5, 7, 4, 1, 3, 0)
 
 
 def attend_kernel(
@@ -244,16 +244,16 @@
         stretch_on_down(j).wait_recv()
 
     def stretch_run(j, _):
-        @pl.when(j == 3)
-        def _():
-            pick(1)
-
         diagonal(j)
 
         def inner(t, _):
             @pl.when((j == 0) & (t == 2))
             def _():
                 forward_stretch(3)
+
+            @pl.when((j == 2) & (t == 3))
+            def _():
+                pick(1)
 
             @pl.when((j == 0) & (t == 3))
             def _():

time: 73.1 us -> 73.1 us (level)
  no operation moved by 1% of the time
where the time goes in v5:
time: 73.1 us; the launch traced here: 73 us
  Pallas kernels  72 us (98%)
  local copies, waits for them, and re-layouts  0.97 us (1%)
    pallas_call x1, Pallas kernels, local(): pl.pallas_call(attend_kernel, out_shape=pltpu.VMEM((128, 4096), BF), in_s...  72 us

profile of v5, /device:TPU:0, one launch (start us, length us, event | category | flops | bytes accessed | tf_op | source)
XLA Modules:
  0.0 73.0 jit_solution(15317853273225722617)
XLA Ops:
  0.0 72.0 %attend.1 = bf16[128,4096]{1,0:T(8,128)(2,1)S(1)} custom-call(bf16[128,4096]{1,0:T(8,128)(2,1)} %bitcast.10, bf16[128,1024]{1,0:T(8,128)(2,1)} %bitcast.13, bf16[128,1024]{1,0:T(8,128)(2,1)} %bitcast.14, bf16[2,128,1024]{2,1,0:T(8,128)(2,1)} %bitcast.11, bf16[2,128,1024]{2,1,0:T(8,128)(2,1)} %bitcast.12, s32[4,32]{1,0:T(4,128)} %bitcast.15, s32[4]{0:T(128)} %plen_ref.1), custom_call_target="tpu_custom_call" | custom-call | flops 14000000000 | bytes 4194304 | tf_op jit(solution)/shard_map/attend/pallas_call | solution.py:378
  72.0 1.0 %copy.9 = bf16[1,128,4096]{2,1,0:T(8,128)(2,1)} copy(bf16[1,128,4096]{2,1,0:T(8,128)(2,1)S(1)} %bitcast.9) | data formatting | bytes 2097152
